TPU v7x, 32 devices: a whole 2x2x4 slice. The times are simulated.
32 devices in a mesh: blk: 8 (over y, x, core), tm: 4 (over z).
Axes of the slice: x: 2, y: 2, z: 4, core: 2. Of those that a mesh axis runs over, the one named last changes fastest.
Arguments:
- records: bfloat16 [2048, 16, 512], P('blk', 'tm'), may hold values from -6 to 6
- glitch_mask: int32 [2048, 16], P('blk'), may hold values 0 or 1
- fir_taps: bfloat16 [65], replicated, may hold values from -1.1953125 to 1.1953125
Outputs:
- correlations: bfloat16 [16, 2048, 2048], P('tm', 'blk')
All inputs are finite; a program needn't handle non-finite values. No bound on the sum of `glitch_mask` on one device may be relied on, other than what follows from the above.
Results may differ from a plain program's by a relative error of at most 0.015.
Values may be sent and summed in bfloat16 or wider, within the bound.
A program may use at most 256 MiB of HBM per device.

v0:
```python
import math

import jax
import jax.numpy as jnp
from jax import lax
from jax.sharding import PartitionSpec as P

BINS = 128
FIRST_BIN = 16
SMOOTH = 64
LAGS = 16


def passed_along(value, axis, steps):
    count = lax.axis_size(axis)
    pairs = [(source, (source + steps) % count) for source in range(count)]
    return lax.ppermute(value, axis, pairs)


def filter_matrix(fir_taps, seglen):
    source = lax.broadcasted_iota(jnp.int32, (seglen, seglen), 0)
    target = lax.broadcasted_iota(jnp.int32, (seglen, seglen), 1)
    offsets = source - target + (fir_taps.shape[0] - 1) // 2
    weights = fir_taps.astype(jnp.float32)
    matrix = jnp.zeros((seglen, seglen), jnp.float32)
    for tap_index in range(fir_taps.shape[0]):
        matrix = matrix + jnp.where(offsets == tap_index, weights[tap_index], jnp.float32(0.0))
    return matrix


def transform_table(fir_taps, seglen):
    sample = lax.broadcasted_iota(jnp.int32, (seglen, BINS), 0)
    freq = lax.broadcasted_iota(jnp.int32, (seglen, BINS), 1) + FIRST_BIN
    phase = sample * freq % seglen
    angle = phase.astype(jnp.float32) * jnp.float32(2.0 * math.pi / seglen)
    dft = jnp.concatenate([jnp.cos(angle), -jnp.sin(angle)], axis=1)
    combined = jnp.dot(
        filter_matrix(fir_taps, seglen),
        dft,
        precision=lax.Precision.HIGHEST,
        preferred_element_type=jnp.float32,
    )
    return combined.astype(jnp.bfloat16)


def whiten(samples, usable, fir_taps):
    seglen = samples.shape[1]
    source = lax.broadcasted_iota(jnp.int32, (seglen, seglen), 0)
    target = lax.broadcasted_iota(jnp.int32, (seglen, seglen), 1)
    inside = jnp.abs(source - target) <= SMOOTH
    band_ones = jnp.where(inside, 1.0, 0.0).astype(jnp.bfloat16)
    counts = jnp.sum(jnp.where(inside, 1.0, 0.0).astype(jnp.float32), axis=0)
    envelope = (
        jnp.dot(jnp.abs(samples), band_ones, preferred_element_type=jnp.float32) / counts[None, :]
    )
    normal = (samples.astype(jnp.float32) / (envelope + 1e-06)).astype(jnp.bfloat16)
    spectra = jnp.dot(normal, transform_table(fir_taps, seglen), preferred_element_type=jnp.float32)
    real_part = spectra[:, :BINS]
    imag_part = spectra[:, BINS:]
    power_mean = jnp.mean(real_part * real_part + imag_part * imag_part, axis=1, keepdims=True)
    scale_rows = usable.astype(jnp.float32)[:, None] / jnp.sqrt(power_mean + 1e-06)
    return (spectra * scale_rows).astype(jnp.bfloat16)


def lag_tables(tm_index, bins_dev, seg_total, seglen):
    delay = lax.broadcasted_iota(jnp.int32, (LAGS, bins_dev), 0) - LAGS // 2
    freq = lax.broadcasted_iota(jnp.int32, (LAGS, bins_dev), 1) + FIRST_BIN + tm_index * bins_dev
    phase = delay * freq % seglen
    angle = phase.astype(jnp.float32) * jnp.float32(2.0 * math.pi / seglen)
    factor = jnp.float32(1.0 / math.sqrt(seg_total * BINS))
    return (
        (jnp.cos(angle) * factor).astype(jnp.bfloat16),
        (jnp.sin(angle) * factor).astype(jnp.bfloat16),
    )


def cross_spectra(left_pair, visitor):
    right_real = jnp.concatenate([visitor[0], visitor[1]], axis=1)
    right_imag = jnp.concatenate([visitor[0], -visitor[1]], axis=1)
    real_part = jnp.einsum(
        "fsi,fsj->fij", left_pair[0], right_real, preferred_element_type=jnp.float32
    )
    imag_part = jnp.einsum(
        "fsi,fsj->fij", left_pair[1], right_imag, preferred_element_type=jnp.float32
    )
    return (real_part.astype(jnp.bfloat16), imag_part.astype(jnp.bfloat16))


def make_pair(spectra):
    return (
        jnp.concatenate([spectra[0], spectra[1]], axis=1),
        jnp.concatenate([spectra[1], spectra[0]], axis=1),
    )


def body(records, glitch_mask, fir_taps):
    tm_count = lax.axis_size("tm")
    cycle_size = lax.axis_size("blk")
    tm_index = lax.axis_index("tm")
    cycle_index = lax.axis_index("blk")
    turned = lax.all_to_all(records, "tm", split_axis=0, concat_axis=1, tiled=True)
    local_chan, seg_total, seglen = turned.shape
    usable = lax.dynamic_slice_in_dim(glitch_mask, tm_index * local_chan, local_chan, 0)
    whitened = whiten(
        turned.reshape(local_chan * seg_total, seglen),
        usable.reshape(local_chan * seg_total),
        fir_taps,
    )
    spectra = jnp.transpose(whitened.reshape(local_chan, seg_total, 2, BINS), (2, 3, 1, 0))
    lags_dev = LAGS // tm_count
    banded = lax.all_to_all(spectra, "tm", split_axis=1, concat_axis=3, tiled=True)
    bins_dev = banded.shape[1]
    block_chan = banded.shape[3]
    left_pair = make_pair(banded)
    cos_rows, sin_rows = lag_tables(tm_index, bins_dev, seg_total, seglen)

    def record(stacked, column, visitor):
        real_part, imag_part = cross_spectra(left_pair, visitor)
        shares = lax.psum_scatter(
            (
                jnp.einsum("lf,fij->lij", cos_rows, real_part, preferred_element_type=jnp.float32)
                - jnp.einsum("lf,fij->lij", sin_rows, imag_part, preferred_element_type=jnp.float32)
            ).astype(jnp.bfloat16),
            "tm",
            scatter_dimension=0,
            tiled=True,
        )
        return lax.dynamic_update_slice_in_dim(stacked, shares, column * block_chan, 2)

    stacked = jnp.zeros((lags_dev, block_chan, block_chan * cycle_size), jnp.bfloat16)
    stacked = record(stacked, cycle_index, banded)

    def one_way(step_index, carry):
        accum, visitor = carry
        visitor = passed_along(visitor, "blk", 1)
        accum = record(accum, (cycle_index - step_index) % cycle_size, visitor)
        return (accum, visitor)

    stacked, visitor = lax.fori_loop(1, cycle_size, one_way, (stacked, banded))
    return stacked


def solution(mesh):
    placed = (P("blk", "tm", None), P("blk", None), P())
    return jax.shard_map(
        body, mesh=mesh, in_specs=placed, out_specs=P("tm", "blk", None), check_vma=False
    )
```

profile of v0, /device:TPU:0, one launch (start us, length us, event | category | flops | bytes accessed | tf_op | source)
XLA Modules:
  0.0 742.8 jit_solution(16734487282435258296)
XLA Ops:
  6.5 6.3 all-to-all-start
  22.8 43.9 %convolution_convert_fusion.2 = bf16[512,256]{1,0:T(8,128)(2,1)S(1)} fusion(f32[512,128]{1,0:T(8,128)S(1)} %get-tuple-element.344, f32[512,128]{1,0:T(8,128)S(1)} %get-tuple-element.343, f32[]{:T(128)} %bitcast.70, f32[]{:T(128)} %bitcast.69, f32[]{:T(128)} %bitcast.68, f32[]{:T(128)} %bitcast.67, f32[]{:T(128)} %bitcast.66, f32[]{:T(128)} %bitcast.65, ...), kind=kOutput, calls=%fused_computation.54 | convolution fusion | flops 856948736 | bytes 786692 | tf_op jit(solution)/shard_map/dot_general | solution.py:37
  78.9 5.1 all-to-all-start.1
  84.0 13.9 %all-to-all-done.1 = bf16[4,2,32768]{2,1,0:T(2,128)(2,1)S(1)} async-done(((bf16[4,2,32768]{2,1,0:T(2,128)(2,1)}), bf16[4,2,32768]{2,1,0:T(2,128)(2,1)S(1)}, u32[]{:S(2)}, u32[]{:S(2)}) %all-to-all-start.1) | async-done | bytes 524320 | tf_op jit(solution)/shard_map/all_to_all | solution.py:111
  112.9 40.9 %reduce-scatter.3.cloned.1.call-done = bf16[4,256,256]{2,1,0:T(8,128)(2,1)} async-done(((bf16[16,256,256]{2,1,0:T(8,128)(2,1)}), bf16[4,256,256]{2,1,0:T(8,128)(2,1)}) %reduce-scatter.3.cloned.1.call-update) | async-done | bytes 524304 | tf_op jit(solution)/shard_map/reduce_scatter | solution.py:119
  156.9 579.0 %while.19 = (s32[]{:T(128)}, bf16[4,256,2048]{2,1,0:T(8,128)(2,1)}, bf16[2,32,16,256]{3,2,1,0:T(8,128)(2,1)S(1)}, bf16[32,32,256]{2,1,0:T(8,128)(2,1)S(1)}, bf16...) while((s32[]{:T(128)}, bf16[4,256,2048]{2,1,0:T(8,128)(2,1)}, ...), condition=%wide.region_5.6_spmd.clone.clone, body=%wide.region_3.5_spmd.clone.clone.sunk | while | flops 411189248 | bytes 80741144 | solution.py:139
  156.9 9.5 %collective-permute-done = bf16[2,32,16,256]{3,2,1,0:T(8,128)(2,1)S(1)} collective-permute-done((bf16[2,32,16,256]{3,2,1,0:T(8,128)(2,1)S(1)}, bf16[2,32,16,256]{3,2,1,0:T(8,128)(2,1)S(1)}, u32[]{:S(2)}, u32[]{:S(2)}) %collective-permute-start) | collective-permute-done | bytes 524320 | tf_op jit(solution)/shard_map/while/body/eval_jaxpr/ppermute | solution.py:17
  166.5 3.3 convert_bitcast_fusion.4
  169.7 7.9 %copy.102 = bf16[32,256,256]{2,0,1:T(8,128)(2,1)} copy(bf16[32,256,256]{1,2,0:T(8,128)(2,1)} %convert_bitcast_fusion.4) | data formatting | bytes 8388608 | tf_op jit(solution)/shard_map/while/body/eval_jaxpr/convert_element_type | solution.py:86
  177.7 3.3 convert_bitcast_fusion.5
  180.9 7.9 %copy.103 = bf16[32,256,256]{2,0,1:T(8,128)(2,1)} copy(bf16[32,256,256]{1,2,0:T(8,128)(2,1)} %convert_bitcast_fusion.5) | data formatting | bytes 8388608 | tf_op jit(solution)/shard_map/while/body/eval_jaxpr/convert_element_type | solution.py:86
  195.4 42.4 %reduce-scatter.5.cloned.1.call-done = bf16[4,256,256]{2,1,0:T(8,128)(2,1)} async-done(((bf16[16,256,256]{2,1,0:T(8,128)(2,1)}), bf16[4,256,256]{2,1,0:T(8,128)(2,1)}) %reduce-scatter.5.cloned.1.call-update) | async-done | bytes 524304 | tf_op jit(solution)/shard_map/while/body/eval_jaxpr/reduce_scatter | solution.py:119
  239.6 9.5 %collective-permute-done = bf16[2,32,16,256]{3,2,1,0:T(8,128)(2,1)S(1)} collective-permute-done((bf16[2,32,16,256]{3,2,1,0:T(8,128)(2,1)S(1)}, bf16[2,32,16,256]{3,2,1,0:T(8,128)(2,1)S(1)}, u32[]{:S(2)}, u32[]{:S(2)}) %collective-permute-start) | collective-permute-done | bytes 524320 | tf_op jit(solution)/shard_map/while/body/eval_jaxpr/ppermute | solution.py:17
  249.2 3.3 convert_bitcast_fusion.4
  252.4 7.9 %copy.102 = bf16[32,256,256]{2,0,1:T(8,128)(2,1)} copy(bf16[32,256,256]{1,2,0:T(8,128)(2,1)} %convert_bitcast_fusion.4) | data formatting | bytes 8388608 | tf_op jit(solution)/shard_map/while/body/eval_jaxpr/convert_element_type | solution.py:86
  260.4 3.3 convert_bitcast_fusion.5
  263.6 7.9 %copy.103 = bf16[32,256,256]{2,0,1:T(8,128)(2,1)} copy(bf16[32,256,256]{1,2,0:T(8,128)(2,1)} %convert_bitcast_fusion.5) | data formatting | bytes 8388608 | tf_op jit(solution)/shard_map/while/body/eval_jaxpr/convert_element_type | solution.py:86
  278.1 42.4 %reduce-scatter.5.cloned.1.call-done = bf16[4,256,256]{2,1,0:T(8,128)(2,1)} async-done(((bf16[16,256,256]{2,1,0:T(8,128)(2,1)}), bf16[4,256,256]{2,1,0:T(8,128)(2,1)}) %reduce-scatter.5.cloned.1.call-update) | async-done | bytes 524304 | tf_op jit(solution)/shard_map/while/body/eval_jaxpr/reduce_scatter | solution.py:119
  322.3 9.5 %collective-permute-done = bf16[2,32,16,256]{3,2,1,0:T(8,128)(2,1)S(1)} collective-permute-done((bf16[2,32,16,256]{3,2,1,0:T(8,128)(2,1)S(1)}, bf16[2,32,16,256]{3,2,1,0:T(8,128)(2,1)S(1)}, u32[]{:S(2)}, u32[]{:S(2)}) %collective-permute-start) | collective-permute-done | bytes 524320 | tf_op jit(solution)/shard_map/while/body/eval_jaxpr/ppermute | solution.py:17
  331.9 3.3 convert_bitcast_fusion.4
  335.1 7.9 %copy.102 = bf16[32,256,256]{2,0,1:T(8,128)(2,1)} copy(bf16[32,256,256]{1,2,0:T(8,128)(2,1)} %convert_bitcast_fusion.4) | data formatting | bytes 8388608 | tf_op jit(solution)/shard_map/while/body/eval_jaxpr/convert_element_type | solution.py:86
  343.1 3.3 convert_bitcast_fusion.5
  346.3 7.9 %copy.103 = bf16[32,256,256]{2,0,1:T(8,128)(2,1)} copy(bf16[32,256,256]{1,2,0:T(8,128)(2,1)} %convert_bitcast_fusion.5) | data formatting | bytes 8388608 | tf_op jit(solution)/shard_map/while/body/eval_jaxpr/convert_element_type | solution.py:86
  360.8 42.4 %reduce-scatter.5.cloned.1.call-done = bf16[4,256,256]{2,1,0:T(8,128)(2,1)} async-done(((bf16[16,256,256]{2,1,0:T(8,128)(2,1)}), bf16[4,256,256]{2,1,0:T(8,128)(2,1)}) %reduce-scatter.5.cloned.1.call-update) | async-done | bytes 524304 | tf_op jit(solution)/shard_map/while/body/eval_jaxpr/reduce_scatter | solution.py:119
  405.1 9.5 %collective-permute-done = bf16[2,32,16,256]{3,2,1,0:T(8,128)(2,1)S(1)} collective-permute-done((bf16[2,32,16,256]{3,2,1,0:T(8,128)(2,1)S(1)}, bf16[2,32,16,256]{3,2,1,0:T(8,128)(2,1)S(1)}, u32[]{:S(2)}, u32[]{:S(2)}) %collective-permute-start) | collective-permute-done | bytes 524320 | tf_op jit(solution)/shard_map/while/body/eval_jaxpr/ppermute | solution.py:17
  414.6 3.3 convert_bitcast_fusion.4
  417.9 7.9 %copy.102 = bf16[32,256,256]{2,0,1:T(8,128)(2,1)} copy(bf16[32,256,256]{1,2,0:T(8,128)(2,1)} %convert_bitcast_fusion.4) | data formatting | bytes 8388608 | tf_op jit(solution)/shard_map/while/body/eval_jaxpr/convert_element_type | solution.py:86
  425.8 3.3 convert_bitcast_fusion.5
  429.1 7.9 %copy.103 = bf16[32,256,256]{2,0,1:T(8,128)(2,1)} copy(bf16[32,256,256]{1,2,0:T(8,128)(2,1)} %convert_bitcast_fusion.5) | data formatting | bytes 8388608 | tf_op jit(solution)/shard_map/while/body/eval_jaxpr/convert_element_type | solution.py:86
  443.6 42.4 %reduce-scatter.5.cloned.1.call-done = bf16[4,256,256]{2,1,0:T(8,128)(2,1)} async-done(((bf16[16,256,256]{2,1,0:T(8,128)(2,1)}), bf16[4,256,256]{2,1,0:T(8,128)(2,1)}) %reduce-scatter.5.cloned.1.call-update) | async-done | bytes 524304 | tf_op jit(solution)/shard_map/while/body/eval_jaxpr/reduce_scatter | solution.py:119
  487.8 9.5 %collective-permute-done = bf16[2,32,16,256]{3,2,1,0:T(8,128)(2,1)S(1)} collective-permute-done((bf16[2,32,16,256]{3,2,1,0:T(8,128)(2,1)S(1)}, bf16[2,32,16,256]{3,2,1,0:T(8,128)(2,1)S(1)}, u32[]{:S(2)}, u32[]{:S(2)}) %collective-permute-start) | collective-permute-done | bytes 524320 | tf_op jit(solution)/shard_map/while/body/eval_jaxpr/ppermute | solution.py:17
  497.3 3.3 convert_bitcast_fusion.4
  500.6 7.9 %copy.102 = bf16[32,256,256]{2,0,1:T(8,128)(2,1)} copy(bf16[32,256,256]{1,2,0:T(8,128)(2,1)} %convert_bitcast_fusion.4) | data formatting | bytes 8388608 | tf_op jit(solution)/shard_map/while/body/eval_jaxpr/convert_element_type | solution.py:86
  508.5 3.3 convert_bitcast_fusion.5
  511.8 7.9 %copy.103 = bf16[32,256,256]{2,0,1:T(8,128)(2,1)} copy(bf16[32,256,256]{1,2,0:T(8,128)(2,1)} %convert_bitcast_fusion.5) | data formatting | bytes 8388608 | tf_op jit(solution)/shard_map/while/body/eval_jaxpr/convert_element_type | solution.py:86
  526.2 42.4 %reduce-scatter.5.cloned.1.call-done = bf16[4,256,256]{2,1,0:T(8,128)(2,1)} async-done(((bf16[16,256,256]{2,1,0:T(8,128)(2,1)}), bf16[4,256,256]{2,1,0:T(8,128)(2,1)}) %reduce-scatter.5.cloned.1.call-update) | async-done | bytes 524304 | tf_op jit(solution)/shard_map/while/body/eval_jaxpr/reduce_scatter | solution.py:119
  570.5 9.5 %collective-permute-done = bf16[2,32,16,256]{3,2,1,0:T(8,128)(2,1)S(1)} collective-permute-done((bf16[2,32,16,256]{3,2,1,0:T(8,128)(2,1)S(1)}, bf16[2,32,16,256]{3,2,1,0:T(8,128)(2,1)S(1)}, u32[]{:S(2)}, u32[]{:S(2)}) %collective-permute-start) | collective-permute-done | bytes 524320 | tf_op jit(solution)/shard_map/while/body/eval_jaxpr/ppermute | solution.py:17
  580.1 3.3 convert_bitcast_fusion.4
  583.3 7.9 %copy.102 = bf16[32,256,256]{2,0,1:T(8,128)(2,1)} copy(bf16[32,256,256]{1,2,0:T(8,128)(2,1)} %convert_bitcast_fusion.4) | data formatting | bytes 8388608 | tf_op jit(solution)/shard_map/while/body/eval_jaxpr/convert_element_type | solution.py:86
  591.3 3.3 convert_bitcast_fusion.5
  594.5 7.9 %copy.103 = bf16[32,256,256]{2,0,1:T(8,128)(2,1)} copy(bf16[32,256,256]{1,2,0:T(8,128)(2,1)} %convert_bitcast_fusion.5) | data formatting | bytes 8388608 | tf_op jit(solution)/shard_map/while/body/eval_jaxpr/convert_element_type | solution.py:86
  609.0 42.4 %reduce-scatter.5.cloned.1.call-done = bf16[4,256,256]{2,1,0:T(8,128)(2,1)} async-done(((bf16[16,256,256]{2,1,0:T(8,128)(2,1)}), bf16[4,256,256]{2,1,0:T(8,128)(2,1)}) %reduce-scatter.5.cloned.1.call-update) | async-done | bytes 524304 | tf_op jit(solution)/shard_map/while/body/eval_jaxpr/reduce_scatter | solution.py:119
  653.2 9.5 %collective-permute-done = bf16[2,32,16,256]{3,2,1,0:T(8,128)(2,1)S(1)} collective-permute-done((bf16[2,32,16,256]{3,2,1,0:T(8,128)(2,1)S(1)}, bf16[2,32,16,256]{3,2,1,0:T(8,128)(2,1)S(1)}, u32[]{:S(2)}, u32[]{:S(2)}) %collective-permute-start) | collective-permute-done | bytes 524320 | tf_op jit(solution)/shard_map/while/body/eval_jaxpr/ppermute | solution.py:17
  662.8 3.3 convert_bitcast_fusion.4
  666.0 7.9 %copy.102 = bf16[32,256,256]{2,0,1:T(8,128)(2,1)} copy(bf16[32,256,256]{1,2,0:T(8,128)(2,1)} %convert_bitcast_fusion.4) | data formatting | bytes 8388608 | tf_op jit(solution)/shard_map/while/body/eval_jaxpr/convert_element_type | solution.py:86
  674.0 3.3 convert_bitcast_fusion.5
  677.2 7.9 %copy.103 = bf16[32,256,256]{2,0,1:T(8,128)(2,1)} copy(bf16[32,256,256]{1,2,0:T(8,128)(2,1)} %convert_bitcast_fusion.5) | data formatting | bytes 8388608 | tf_op jit(solution)/shard_map/while/body/eval_jaxpr/convert_element_type | solution.py:86
  691.7 42.4 %reduce-scatter.5.cloned.1.call-done = bf16[4,256,256]{2,1,0:T(8,128)(2,1)} async-done(((bf16[16,256,256]{2,1,0:T(8,128)(2,1)}), bf16[4,256,256]{2,1,0:T(8,128)(2,1)}) %reduce-scatter.5.cloned.1.call-update) | async-done | bytes 524304 | tf_op jit(solution)/shard_map/while/body/eval_jaxpr/reduce_scatter | solution.py:119
  (136 shorter events, 98.6 us)
Async XLA Ops:
  6.5 60.2 %all-to-all-start = ((bf16[256,4,512]{2,1,0:T(4,128)(2,1)}), bf16[256,4,512]{2,1,0:T(4,128)(2,1)S(1)}, u32[]{:S(2)}, u32[]{:S(2)}) async-start(bf16[256,4,512]{2,1,0:T(4,128)(2,1)} %param.5), calls=%async_computation.1 | async-start | bytes 2097152 | tf_op jit(solution)/shard_map/all_to_all | solution.py:101
  78.9 19.0 %all-to-all-start.1 = ((bf16[4,2,32768]{2,1,0:T(2,128)(2,1)}), bf16[4,2,32768]{2,1,0:T(2,128)(2,1)S(1)}, u32[]{:S(2)}, u32[]{:S(2)}) async-start(bf16[4,2,32768]{2,1,0:T(2,128)(2,1)} %reshape.40), calls=%async_computation.2 | async-start | bytes 1048576 | tf_op jit(solution)/shard_map/all_to_all | solution.py:111
  84.0 69.8 %reduce-scatter.3.cloned.1.call-start = ((), (), s32[]{:S(2)}) async-start(), calls=%async_computation.4 | async-start | bytes 2621440 | tf_op jit(solution)/shard_map/reduce_scatter | solution.py:119
  153.8 1.0 copy-start.2
  154.9 2.0 copy-start.1
  156.9 80.8 %reduce-scatter.5.cloned.1.call-start = ((), (), s32[]{:S(2)}) async-start(), calls=%async_computation.5 | async-start | bytes 2621440 | tf_op jit(solution)/shard_map/while/body/eval_jaxpr/reduce_scatter | solution.py:119
  156.9 9.5 %collective-permute-start = (bf16[2,32,16,256]{3,2,1,0:T(8,128)(2,1)S(1)}, bf16[2,32,16,256]{3,2,1,0:T(8,128)(2,1)S(1)}, u32[]{:S(2)}, u32[]{:S(2)}) collective-permute-start(bf16[2,32,16,256]{3,2,1,0:T(8,128)(2,1)S(1)} %get-tuple-element.414), channel_id=1, source_target_pairs={{0,4},{4,8},{8,12},{12,16},{16,20},{20,24},{24,28},{28,0},{1,5},{5... | collective-permute-start | bytes 1572872 | tf_op jit(solution)/shard_map/while/body/eval_jaxpr/ppermute | solution.py:17
  188.9 3.4 copy-start
  239.6 80.8 %reduce-scatter.5.cloned.1.call-start = ((), (), s32[]{:S(2)}) async-start(), calls=%async_computation.5 | async-start | bytes 2621440 | tf_op jit(solution)/shard_map/while/body/eval_jaxpr/reduce_scatter | solution.py:119
  239.6 9.5 %collective-permute-start = (bf16[2,32,16,256]{3,2,1,0:T(8,128)(2,1)S(1)}, bf16[2,32,16,256]{3,2,1,0:T(8,128)(2,1)S(1)}, u32[]{:S(2)}, u32[]{:S(2)}) collective-permute-start(bf16[2,32,16,256]{3,2,1,0:T(8,128)(2,1)S(1)} %get-tuple-element.414), channel_id=1, source_target_pairs={{0,4},{4,8},{8,12},{12,16},{16,20},{20,24},{24,28},{28,0},{1,5},{5... | collective-permute-start | bytes 1572872 | tf_op jit(solution)/shard_map/while/body/eval_jaxpr/ppermute | solution.py:17
  271.6 3.4 copy-start
  322.3 80.9 %reduce-scatter.5.cloned.1.call-start = ((), (), s32[]{:S(2)}) async-start(), calls=%async_computation.5 | async-start | bytes 2621440 | tf_op jit(solution)/shard_map/while/body/eval_jaxpr/reduce_scatter | solution.py:119
  322.3 9.5 %collective-permute-start = (bf16[2,32,16,256]{3,2,1,0:T(8,128)(2,1)S(1)}, bf16[2,32,16,256]{3,2,1,0:T(8,128)(2,1)S(1)}, u32[]{:S(2)}, u32[]{:S(2)}) collective-permute-start(bf16[2,32,16,256]{3,2,1,0:T(8,128)(2,1)S(1)} %get-tuple-element.414), channel_id=1, source_target_pairs={{0,4},{4,8},{8,12},{12,16},{16,20},{20,24},{24,28},{28,0},{1,5},{5... | collective-permute-start | bytes 1572872 | tf_op jit(solution)/shard_map/while/body/eval_jaxpr/ppermute | solution.py:17
  354.3 3.4 copy-start
  405.1 80.8 %reduce-scatter.5.cloned.1.call-start = ((), (), s32[]{:S(2)}) async-start(), calls=%async_computation.5 | async-start | bytes 2621440 | tf_op jit(solution)/shard_map/while/body/eval_jaxpr/reduce_scatter | solution.py:119
  405.1 9.5 %collective-permute-start = (bf16[2,32,16,256]{3,2,1,0:T(8,128)(2,1)S(1)}, bf16[2,32,16,256]{3,2,1,0:T(8,128)(2,1)S(1)}, u32[]{:S(2)}, u32[]{:S(2)}) collective-permute-start(bf16[2,32,16,256]{3,2,1,0:T(8,128)(2,1)S(1)} %get-tuple-element.414), channel_id=1, source_target_pairs={{0,4},{4,8},{8,12},{12,16},{16,20},{20,24},{24,28},{28,0},{1,5},{5... | collective-permute-start | bytes 1572872 | tf_op jit(solution)/shard_map/while/body/eval_jaxpr/ppermute | solution.py:17
  437.0 3.4 copy-start
  487.8 80.9 %reduce-scatter.5.cloned.1.call-start = ((), (), s32[]{:S(2)}) async-start(), calls=%async_computation.5 | async-start | bytes 2621440 | tf_op jit(solution)/shard_map/while/body/eval_jaxpr/reduce_scatter | solution.py:119
  487.8 9.5 %collective-permute-start = (bf16[2,32,16,256]{3,2,1,0:T(8,128)(2,1)S(1)}, bf16[2,32,16,256]{3,2,1,0:T(8,128)(2,1)S(1)}, u32[]{:S(2)}, u32[]{:S(2)}) collective-permute-start(bf16[2,32,16,256]{3,2,1,0:T(8,128)(2,1)S(1)} %get-tuple-element.414), channel_id=1, source_target_pairs={{0,4},{4,8},{8,12},{12,16},{16,20},{20,24},{24,28},{28,0},{1,5},{5... | collective-permute-start | bytes 1572872 | tf_op jit(solution)/shard_map/while/body/eval_jaxpr/ppermute | solution.py:17
  519.7 3.4 copy-start
  570.5 80.8 %reduce-scatter.5.cloned.1.call-start = ((), (), s32[]{:S(2)}) async-start(), calls=%async_computation.5 | async-start | bytes 2621440 | tf_op jit(solution)/shard_map/while/body/eval_jaxpr/reduce_scatter | solution.py:119
  570.5 9.5 %collective-permute-start = (bf16[2,32,16,256]{3,2,1,0:T(8,128)(2,1)S(1)}, bf16[2,32,16,256]{3,2,1,0:T(8,128)(2,1)S(1)}, u32[]{:S(2)}, u32[]{:S(2)}) collective-permute-start(bf16[2,32,16,256]{3,2,1,0:T(8,128)(2,1)S(1)} %get-tuple-element.414), channel_id=1, source_target_pairs={{0,4},{4,8},{8,12},{12,16},{16,20},{20,24},{24,28},{28,0},{1,5},{5... | collective-permute-start | bytes 1572872 | tf_op jit(solution)/shard_map/while/body/eval_jaxpr/ppermute | solution.py:17
  602.5 3.4 copy-start
  653.2 80.8 %reduce-scatter.5.cloned.1.call-start = ((), (), s32[]{:S(2)}) async-start(), calls=%async_computation.5 | async-start | bytes 2621440 | tf_op jit(solution)/shard_map/while/body/eval_jaxpr/reduce_scatter | solution.py:119
  653.2 9.5 %collective-permute-start = (bf16[2,32,16,256]{3,2,1,0:T(8,128)(2,1)S(1)}, bf16[2,32,16,256]{3,2,1,0:T(8,128)(2,1)S(1)}, u32[]{:S(2)}, u32[]{:S(2)}) collective-permute-start(bf16[2,32,16,256]{3,2,1,0:T(8,128)(2,1)S(1)} %get-tuple-element.414), channel_id=1, source_target_pairs={{0,4},{4,8},{8,12},{12,16},{16,20},{20,24},{24,28},{28,0},{1,5},{5... | collective-permute-start | bytes 1572872 | tf_op jit(solution)/shard_map/while/body/eval_jaxpr/ppermute | solution.py:17
  685.2 3.4 copy-start
Sparse Core Ops, SparseCore 0:
  110.8 42.9 reduce-scatter.2
  195.4 42.2 reduce-scatter.4
  278.1 42.2 reduce-scatter.4
  360.8 42.3 reduce-scatter.4
  443.6 42.2 reduce-scatter.4
  526.3 42.3 reduce-scatter.4
  609.0 42.2 reduce-scatter.4
  691.7 42.2 reduce-scatter.4
where the time goes:
time: 746 us; the launch traced here: 743 us
  waiting for transfers between devices  418 us (56%)
  local copies, waits for them, and re-layouts  168 us (23%)
  matrix products  128 us (17%)
  between operations  13.6 us (2%)
  starting transfers between devices  11.4 us (2%)
    reduce_scatter x8, waiting for transfers between devices, record(): lax.psum_scatter((jnp.einsum('lf,fij->lij', cos_rows, real_part, preferre...  338 us
    convert_element_type x14, local copies, waits for them, and re-layouts, cross_spectra(): return (real_part.astype(jnp.bfloat16), imag_part.astype(jnp.bfloat16))  111 us
    ppermute x7, waiting for transfers between devices, passed_along(): return lax.ppermute(value, axis, pairs)  66.5 us
    dot_general x1, matrix products, transform_table(): jnp.dot(filter_matrix(fir_taps, seglen), dft, precision=lax.Precision.HIG...  43.9 us
    dot_general x8, matrix products, record(): jnp.einsum('lf,fij->lij', cos_rows, real_part, preferred_element_type=jnp...  24.6 us
    dot_general x8, matrix products, cross_spectra(): jnp.einsum('fsi,fsj->fij', left_pair[0], right_real, preferred_element_ty...  24.2 us
    dot_general x8, matrix products, cross_spectra(): jnp.einsum('fsi,fsj->fij', left_pair[1], right_imag, preferred_element_ty...  24.1 us
    convert_element_type x8, local copies, waits for them, and re-layouts, record(): shares = lax.psum_scatter((jnp.einsum('lf,fij->lij', cos_rows, real_part,...  16.6 us
  transfers between devices with their start and end apart: 17, of which 16 were waited for; matrix products, arithmetic and copies ran while one was open for 7% of the time, Pallas kernels for 0%

commit v1 on v0

v1 whole, which is shorter than its diff:
```python
import math

import jax
import jax.numpy as jnp
import numpy as np
from jax import lax
from jax.sharding import PartitionSpec as P

BINS = 128
FIRST_BIN = 16
SMOOTH = 64
LAGS = 16


def dft_thirds(seglen):
    sample = np.arange(seglen)[:, None]
    freq = np.arange(BINS)[None, :] + FIRST_BIN
    angle = (sample * freq % seglen) * (2.0 * math.pi / seglen)
    rest = np.concatenate([np.cos(angle), -np.sin(angle)], axis=1).astype(np.float32)
    thirds = []
    for _ in range(3):
        part = rest.astype(jnp.bfloat16)
        thirds.append(part)
        rest = rest - part.astype(np.float32)
    return np.concatenate(thirds, axis=1)


def lag_rows(seg_total, seglen):
    delay = np.arange(LAGS)[:, None] - LAGS // 2
    freq = np.arange(BINS)[None, :] + FIRST_BIN
    angle = (delay * freq % seglen) * (2.0 * math.pi / seglen)
    factor = 1.0 / math.sqrt(seg_total * BINS)
    tables = np.stack([np.cos(angle), np.sin(angle)]).astype(np.float32) * np.float32(factor)
    return tables.astype(jnp.bfloat16).astype(np.float32)


def filter_matrix(fir_taps, seglen):
    half = (fir_taps.shape[0] - 1) // 2
    period = 2 * seglen
    line = jnp.pad(fir_taps[::-1], (seglen - 1 - half, seglen - half))
    rows = jnp.tile(line, seglen)[: seglen * (period - 1)].reshape(seglen, period - 1)
    return rows[:, seglen - 1 :]


def transform_table(fir_taps, seglen):
    parts = jnp.dot(
        filter_matrix(fir_taps, seglen),
        jnp.asarray(dft_thirds(seglen)),
        preferred_element_type=jnp.float32,
    )
    width = 2 * BINS
    total = parts[:, :width] + (parts[:, width : 2 * width] + parts[:, 2 * width :])
    return total.astype(jnp.bfloat16)


def whiten(samples, usable, fir_taps):
    seglen = samples.shape[1]
    source = lax.broadcasted_iota(jnp.int32, (seglen, seglen), 0)
    target = lax.broadcasted_iota(jnp.int32, (seglen, seglen), 1)
    band_ones = jnp.where(jnp.abs(source - target) <= SMOOTH, 1.0, 0.0).astype(jnp.bfloat16)
    where = lax.broadcasted_iota(jnp.int32, (1, seglen), 1)
    counts = jnp.minimum(where, SMOOTH) + jnp.minimum(seglen - 1 - where, SMOOTH) + 1
    envelope = jnp.dot(
        jnp.abs(samples), band_ones, preferred_element_type=jnp.float32
    ) / counts.astype(jnp.float32)
    normal = (samples.astype(jnp.float32) / (envelope + 1e-06)).astype(jnp.bfloat16)
    spectra = jnp.dot(normal, transform_table(fir_taps, seglen), preferred_element_type=jnp.float32)
    power = jnp.sum(spectra * spectra, axis=1, keepdims=True) * jnp.float32(1.0 / BINS)
    scale = usable.astype(jnp.float32)[:, None] / jnp.sqrt(power + 1e-06)
    return (spectra * scale).astype(jnp.bfloat16)


def body(records, glitch_mask, fir_taps):
    tm_count = lax.axis_size("tm")
    tm_index = lax.axis_index("tm")
    chans, segs, seglen = records.shape
    seg_total = glitch_mask.shape[1]
    usable = lax.dynamic_slice_in_dim(glitch_mask, tm_index * segs, segs, 1)
    white = whiten(records.reshape(chans * segs, seglen), usable.reshape(chans * segs), fir_taps)
    slab = white.reshape(chans, segs * 2 * BINS)
    column = lax.all_gather(slab, "tm", axis=1, tiled=True)
    every = lax.all_gather(column, "blk", axis=0, tiled=True)
    lags_dev = LAGS // tm_count
    tables = lax.dynamic_slice_in_dim(
        jnp.asarray(lag_rows(seg_total, seglen)), tm_index * lags_dev, lags_dev, 1
    )
    cos_rows = tables[0][:, None, None, :]
    sin_rows = tables[1][:, None, None, :]
    own = column.reshape(chans, seg_total, 2, BINS).astype(jnp.float32)
    real_part, imag_part = own[None, :, :, 0], own[None, :, :, 1]
    turned = jnp.stack(
        [cos_rows * real_part - sin_rows * imag_part, cos_rows * imag_part + sin_rows * real_part],
        axis=3,
    ).astype(jnp.bfloat16)
    left = turned.reshape(lags_dev, chans, seg_total * 2 * BINS)
    return jnp.einsum("lik,jk->lij", left, every, preferred_element_type=jnp.float32).astype(
        jnp.bfloat16
    )


def solution(mesh):
    placed = (P("blk", "tm", None), P("blk", None), P())
    return jax.shard_map(
        body, mesh=mesh, in_specs=placed, out_specs=P("tm", "blk", None), check_vma=False
    )
```

time: 746 us -> 193 us (0.26)
  waiting for transfers between devices: 418 us -> 68 us
  local copies, waits for them, and re-layouts: 168 us -> 40.2 us
  matrix products: 128 us -> 28.6 us
  other arithmetic: 3.51 us -> 41.5 us
  starting transfers between devices: 11.4 us -> 0.22 us
    reduce_scatter x8 -> x0, waiting for transfers between devices: 338 us -> none  [record(): lax.psum_scatter((jnp.einsum('lf,fij->lij', cos_rows, real_part, preferre...]
    convert_element_type x25 -> x5, local copies, waits for them, and re-layouts: 128 us -> 21.6 us  [the longest x1 14.5 us: body(): turned = jnp.stack([cos_rows * real_part - sin_rows * imag_part, cos_rows...]
    dot_general x33 -> x2, matrix products: 125 us -> 25.5 us  [the longest x1 23.8 us: body(): jnp.einsum('lik,jk->lij', left, every, preferred_element_type=jnp.float32)]
    all_gather x0 -> x2, waiting for transfers between devices: none -> 67.9 us  [the longest x1 48.6 us: body(): column = lax.all_gather(slab, 'tm', axis=1, tiled=True)]
    ppermute x7 -> x0, waiting for transfers between devices: 66.5 us -> none  [passed_along(): return lax.ppermute(value, axis, pairs)]
    another operation x0 -> x2, other arithmetic: none -> 39 us  [the longest x1 20.3 us: body(): jnp.stack([cos_rows * real_part - sin_rows * imag_part, cos_rows * imag_p...]
    all_to_all x2 -> x0, waiting for transfers between devices: 13.9 us -> none  [the longest x1 13.9 us: body(): lax.all_to_all(spectra, 'tm', split_axis=1, concat_axis=3, tiled=True)]
    dynamic_update_slice x8 -> x0, local copies, waits for them, and re-layouts: 13.1 us -> none  [record(): lax.dynamic_update_slice_in_dim(stacked, shares, column * block_chan, 2)]
  transfers between devices with their start and end apart: 17 -> 2, of which waited for: 16 -> 2; matrix products, arithmetic and copies ran while one was open for 7% -> 37% of each run, Pallas kernels for 0% -> 0%
where the time goes in v1:
time: 193 us; the launch traced here: 192 us
  waiting for transfers between devices  68 us (35%)
  other arithmetic  41.5 us (22%)
  local copies, waits for them, and re-layouts  40.2 us (21%)
  matrix products  28.6 us (15%)
  between operations  13.5 us (7%)
    all_gather x1, waiting for transfers between devices, body(): column = lax.all_gather(slab, 'tm', axis=1, tiled=True)  48.6 us
    dot_general x1, matrix products, body(): jnp.einsum('lik,jk->lij', left, every, preferred_element_type=jnp.float32)  23.8 us
    another operation x1, other arithmetic, body(): jnp.stack([cos_rows * real_part - sin_rows * imag_part, cos_rows * imag_p...  20.3 us
    all_gather x1, waiting for transfers between devices, body(): every = lax.all_gather(column, 'blk', axis=0, tiled=True)  19.4 us
    another operation x1, other arithmetic  18.6 us
    convert_element_type x1, local copies, waits for them, and re-layouts, body(): turned = jnp.stack([cos_rows * real_part - sin_rows * imag_part, cos_rows...  14.5 us
    slice x1, local copies, waits for them, and re-layouts, body(): real_part, imag_part = (own[None, :, :, 0], own[None, :, :, 1])  10.3 us
    convert_element_type x1, local copies, waits for them, and re-layouts, body(): own = column.reshape(chans, seg_total, 2, BINS).astype(jnp.float32)  6.6 us
  transfers between devices with their start and end apart: 2, of which 2 were waited for; matrix products, arithmetic and copies ran while one was open for 37% of the time, Pallas kernels for 0%

profile of v1, /device:TPU:0, one launch (start us, length us, event | category | flops | bytes accessed | tf_op | source)
XLA Modules:
  0.0 192.0 jit_solution(9935563108440876466)
XLA Ops:
  6.5 0.0 all-gather.3.cloned.1.call-start
  6.5 1.8 abs.10
  8.3 2.4 %reshape.75 = f32[1024,512]{1,0:T(8,128)} reshape(bf16[256,4,512]{2,1,0:T(4,128)(2,1)} %param.5) | data formatting | bytes 3145728 | tf_op jit(solution)/shard_map/convert_element_type | solution.py:66
  10.7 0.7 dynamic-slice_convert_fusion
  11.4 0.1 copy.6
  11.6 0.1 convert_element_type.59
  11.7 0.7 rev.3
  12.5 0.1 pad.4
  12.5 0.2 broadcast_bitcast_fusion
  12.8 0.3 copy.8
  13.1 1.6 reshape.73
  14.7 1.1 abs.11
  15.8 1.7 fusion.11
  17.6 3.1 %multiply_reduce_fusion = (f32[1024]{0:T(1024)S(1)}, f32[1024,256]{0,1:T(8,128)S(1)}) fusion(f32[512,768]{1,0:T(8,128)S(1)} %fusion.11, f32[1024,512]{1,0:T(8,128)} %reshape.75, bf16[1024,512]{1,0:T(8,128)(2,1)} %abs.11, f32[512]{0:T(512)S(1)} %fusion.22), kind=kOutput, calls=%fused_computation.10 | convolution fusion | flops 809630720 | bytes 5773312 | tf_op jit(solution)/shard_map/dot_general | solution.py:67
  20.7 0.1 multiply_convert_fusion
  20.8 0.2 copy.7
  21.0 1.1 reshape.74
  22.1 0.0 all-gather.3.cloned.1.call-update
  22.1 0.2 all-gather.5.cloned.1.call-start
  22.3 48.6 %all-gather.3.cloned.1.call-done = bf16[256,4096]{1,0:T(8,128)(2,1)} async-done(((bf16[256,1024]{1,0:T(8,128)(2,1)}), bf16[256,4096]{1,0:T(8,128)(2,1)}) %all-gather.3.cloned.1.call-update) | async-done | bytes 2097168 | tf_op jit(solution)/shard_map/all_gather | solution.py:81
  70.9 0.0 all-gather.5.cloned.1.call-update
  70.9 0.7 dynamic-slice_bitcast_fusion.1
  71.7 6.6 %reshape.76 = f32[256,16,2,128]{3,2,1,0:T(2,128)} reshape(bf16[256,4096]{1,0:T(8,128)(2,1)} %all-gather.3.cloned.1.call-done) | data formatting | bytes 6291456 | tf_op jit(solution)/shard_map/convert_element_type | solution.py:89
  78.2 10.3 %fusion.31 = (f32[256,16,1,128]{3,2,1,0:T(1,128)S(1)}, f32[256,16,1,128]{3,2,1,0:T(1,128)}) fusion(f32[256,16,2,128]{3,2,1,0:T(2,128)} %reshape.76), kind=kLoop, calls=%fused_computation.38 | loop fusion | bytes 8388608 | tf_op jit(solution)/shard_map/slice | solution.py:90
  88.5 18.6 %subtract_convert_fusion = (bf16[4,256,16,1,128]{4,3,2,1,0:T(2,128)(2,1)S(1)}, bf16[4,256,16,1,128]{4,3,2,1,0:T(2,128)(2,1)S(1)}) fusion(f32[256,16,128]{2,1,0:T(8,128)} %bitcast.27, f32[4,128]{1,0:T(4,128)S(1)} %get-tuple-element.10, f32[256,16,128]{2,1,0:T(8,128)S(1)} %bitcast.26, f32[4,128]{1,0:T(4,128)S(1)} %get-tuple-element.9), kind=kLoop, calls=%fused_computation.4 | loop fusion | flops 16777216 | bytes 12587008 | tf_op jit(solution)/shard_map/convert.2
  107.2 20.3 %pad_maximum_fusion = bf16[4,256,16,2,128]{4,3,2,1,0:T(2,128)(2,1)} fusion(bf16[4,256,16,1,128]{4,3,2,1,0:T(2,128)(2,1)S(1)} %get-tuple-element.6, bf16[4,256,16,1,128]{4,3,2,1,0:T(2,128)(2,1)S(1)} %get-tuple-element.5), kind=kLoop, calls=%fused_computation.2 | loop fusion | flops 16777216 | bytes 16777216 | tf_op jit(solution)/shard_map/stack | solution.py:91
  127.5 14.5 %convert_element_type.63 = bf16[4,256,4096]{2,1,0:T(8,128)(2,1)} reshape(bf16[4,256,16,2,128]{4,3,2,1,0:T(2,128)(2,1)} %pad_maximum_fusion) | data formatting | bytes 16777216 | tf_op jit(solution)/shard_map/convert_element_type | solution.py:94
  142.0 19.4 %all-gather.5.cloned.1.call-done = bf16[2048,4096]{1,0:T(8,128)(2,1)} async-done(((bf16[256,4096]{1,0:T(8,128)(2,1)}), bf16[2048,4096]{1,0:T(8,128)(2,1)}) %all-gather.5.cloned.1.call-update) | async-done | bytes 16777232 | tf_op jit(solution)/shard_map/all_gather | solution.py:82
  161.4 23.8 %fusion.2 = bf16[4,256,2048]{2,1,0:T(8,128)(2,1)} fusion(bf16[4,256,4096]{2,1,0:T(8,128)(2,1)} %convert_element_type.63, bf16[2048,4096]{1,0:T(8,128)(2,1)} %all-gather.5.cloned.1.call-done), kind=kOutput, calls=%fused_computation.5 | convolution fusion | flops 17181966336 | bytes 29360128 | tf_op jit(solution)/shard_map/lik,jk->lij/dot_general | solution.py:96
  (2 shorter events, 0.0 us)
Async XLA Ops:
  6.5 64.4 %all-gather.3.cloned.1.call-start = ((), (), s32[]{:S(2)}) async-start(), calls=%async_computation | async-start | bytes 2621440 | tf_op jit(solution)/shard_map/all_gather | solution.py:81
  22.1 139.3 %all-gather.5.cloned.1.call-start = ((), (), s32[]{:S(2)}) async-start(), calls=%async_computation.1 | async-start | bytes 18874368 | tf_op jit(solution)/shard_map/all_gather | solution.py:82
Sparse Core Ops, SparseCore 0:
  22.2 48.6 all-gather.2
  72.8 88.5 all-gather.4

commit v2 on v1

--- a/solution.py
+++ b/solution.py
@@ -4,6 +4,8 @@
 import jax.numpy as jnp
 import numpy as np
 from jax import lax
+from jax.experimental import pallas as pl
+from jax.experimental.pallas import tpu as pltpu
 from jax.sharding import PartitionSpec as P
 
 BINS = 128
@@ -70,7 +72,7 @@
     return (spectra * scale).astype(jnp.bfloat16)
 
 
-def body(records, glitch_mask, fir_taps):
+def gathered_body(records, glitch_mask, fir_taps):
     tm_count = lax.axis_size("tm")
     tm_index = lax.axis_index("tm")
     chans, segs, seglen = records.shape
@@ -98,8 +100,265 @@
     )
 
 
+NEAREST = ((0, 1, 2, 3), (1, 2, 0, 3), (2, 1, 3, 0), (3, 2, 1, 0))
+MESH = pl.DeviceIdType.MESH
+
+
+def kernel(x_ref, use_ref, line_ref, dft_ref, tab_ref, out_ref, slabs, left, acc, done, sent, got, outs):
+    segs, chans, seglen = x_ref.shape
+    width = 2 * BINS
+    depth = segs * width
+    lags = left.shape[1]
+    half = chans // 2
+    b, z = lax.axis_index("blk"), lax.axis_index("tm")
+    core = lax.rem(b, 2)
+    at_x = lax.rem(lax.div(b, 2), 2)
+    at_y = lax.div(b, 4)
+    sib = b + 1 - 2 * core
+    by_x = b + 2 - 4 * at_x
+    by_y = b + 4 - 8 * at_y
+    across = by_x + 4 - 8 * at_y
+    up, down = z + 1, z - 1
+    has_up, has_down = z < 3, z > 0
+
+    barrier = pltpu.get_barrier_semaphore()
+    for peer in (sib, by_x, by_y):
+        pl.semaphore_signal(barrier, inc=1, device_id=(peer, z), device_id_type=MESH)
+
+    @pl.when(has_up)
+    def _():
+        pl.semaphore_signal(barrier, inc=1, device_id=(b, up), device_id_type=MESH)
+
+    @pl.when(has_down)
+    def _():
+        pl.semaphore_signal(barrier, inc=1, device_id=(b, down), device_id_type=MESH)
+
+    def slab_of(plane, block):
+        return plane * 8 + block
+
+    own = slab_of(z, b)
+    line = jnp.broadcast_to(line_ref[...], (seglen, 2 * seglen))
+    fir = pltpu.roll(line, 0, 1, stride=1, stride_axis=0)[:, :seglen].astype(jnp.bfloat16)
+    parts = jnp.dot(fir, dft_ref[...], preferred_element_type=jnp.float32)
+    table = (parts[:, :width] + (parts[:, width : 2 * width] + parts[:, 2 * width :])).astype(jnp.bfloat16)
+    source = lax.broadcasted_iota(jnp.int32, (seglen, seglen), 0)
+    target = lax.broadcasted_iota(jnp.int32, (seglen, seglen), 1)
+    band_ones = jnp.where(jnp.abs(source - target) <= SMOOTH, 1.0, 0.0).astype(jnp.bfloat16)
+    where = lax.broadcasted_iota(jnp.int32, (1, seglen), 1)
+    counts = jnp.minimum(where, SMOOTH) + jnp.minimum(seglen - 1 - where, SMOOTH) + 1
+    counts = counts.astype(jnp.float32)
+    for s in range(segs):
+        samples = x_ref[s]
+        envelope = jnp.dot(jnp.abs(samples), band_ones, preferred_element_type=jnp.float32) / counts
+        normal = (samples.astype(jnp.float32) / (envelope + 1e-06)).astype(jnp.bfloat16)
+        spectra = jnp.dot(normal, table, preferred_element_type=jnp.float32)
+        power = jnp.sum(spectra * spectra, axis=1, keepdims=True) * jnp.float32(1.0 / BINS)
+        scale = use_ref[:, s : s + 1] / jnp.sqrt(power + 1e-06)
+        slabs[own, :, s * width : (s + 1) * width] = (spectra * scale).astype(jnp.bfloat16)
+
+    pl.semaphore_wait(barrier, 3 + has_up.astype(jnp.int32) + has_down.astype(jnp.int32))
+
+    sends = []
+
+    def view(slab, part):
+        if part is None:
+            return slabs.at[slab], got.at[slab, 0]
+        return slabs.at[slab, pl.ds(part * half, half)], got.at[slab, part]
+
+    def send(slab, block, plane, part=None, when=None):
+        ref, sem = view(slab, part)
+        copy = pltpu.make_async_remote_copy(
+            src_ref=ref, dst_ref=ref, send_sem=sent.at[len(sends)], recv_sem=sem,
+            device_id=(block, plane), device_id_type=MESH,
+        )
+        sends.append((copy, when))
+        if when is None:
+            copy.start()
+        else:
+            pl.when(when)(copy.start)
+
+    def arrive(slab, part=None):
+        ref, sem = view(slab, part)
+        pltpu.make_async_remote_copy(
+            src_ref=ref, dst_ref=ref, send_sem=sent.at[0], recv_sem=sem,
+            device_id=(sib, z), device_id_type=MESH,
+        ).wait_recv()
+
+    plane_at, onward, goes_on = [z], [None], [None]
+    for step in range(1, 4):
+        plane = sum(jnp.where(z == at, NEAREST[at][step], 0) for at in range(4))
+        following = jnp.where(plane > z, z - 1, z + 1)
+        plane_at.append(plane)
+        onward.append(following)
+        goes_on.append(jnp.logical_and(following >= 0, following <= 3))
+
+    def turn(step):
+        slab = slab_of(plane_at[step], b)
+
+        def one(lag, carry):
+            row = z * lags + lag
+            cos_row = tab_ref[0, pl.ds(row, 1), :]
+            sin_row = tab_ref[1, pl.ds(row, 1), :]
+            for s in range(segs):
+                at = s * width
+                real_part = slabs[slab, :, at : at + BINS].astype(jnp.float32)
+                imag_part = slabs[slab, :, at + BINS : at + width].astype(jnp.float32)
+                left[step, lag, :, at : at + BINS] = (
+                    cos_row * real_part - sin_row * imag_part
+                ).astype(jnp.bfloat16)
+                left[step, lag, :, at + BINS : at + width] = (
+                    cos_row * imag_part + sin_row * real_part
+                ).astype(jnp.bfloat16)
+            return carry
+
+        lax.fori_loop(0, lags, one, 0)
+
+    copies = []
+
+    def correlate(step, block):
+        pair = lax.div(block, 2)
+        first_slab = slab_of(plane_at[step], pair * 2)
+        columns = pl.ds(pl.multiple_of(pair * 2 * chans, 2 * chans), 2 * chans)
+
+        def one(lag, carry):
+            right = slabs[pl.ds(first_slab, 2)].reshape(2 * chans, depth)
+            term = lax.dot_general(
+                left[step, lag], right, (((1,), (1,)), ((), ())), preferred_element_type=jnp.float32
+            )
+            if step == 0:
+                acc[lag, :, columns] = term
+            elif step < 3:
+                acc[lag, :, columns] += term
+            else:
+                done[lag, :, columns] = (acc[lag, :, columns] + term).astype(jnp.bfloat16)
+            return carry
+
+        lax.fori_loop(0, lags, one, 0)
+        if step == 3:
+            copy = pltpu.make_async_copy(
+                done.at[:, :, columns], out_ref.at[:, :, columns], outs.at[len(copies)]
+            )
+            copy.start()
+            copies.append(copy)
+
+    def other_core(block):
+        return block + 1 - 2 * core
+
+    send(own, b, up, when=has_up)
+    send(own, b, down, when=has_down)
+    send(own, by_x, z)
+    send(own, by_y, z)
+    send(own, sib, z)
+    turn(0)
+
+    def corner(step):
+        slab = slab_of(plane_at[step], across)
+        if step in (0, 3):
+            arrive(slab, 0)
+            arrive(slab, 1)
+        else:
+            arrive(slab)
+        if step == 0:
+            send(slab, b, up, when=has_up)
+            send(slab, b, down, when=has_down)
+        elif step == 1:
+            send(slab, b, onward[1], when=goes_on[1])
+        send(slab, sib, z)
+        arrive(slab_of(plane_at[step], other_core(across)))
+        correlate(step, across)
+
+    for step in range(4):
+        plane = plane_at[step]
+        if step < 3:
+            slab = slab_of(plane_at[step + 1], b)
+            arrive(slab)
+            send(slab, b, onward[step + 1], when=goes_on[step + 1])
+            send(slab, by_x, z)
+            send(slab, by_y, z)
+            send(slab, sib, z)
+        slab = slab_of(plane, by_x)
+        arrive(slab)
+        if step in (0, 3):
+            send(slab, by_y, z, part=0)
+        send(slab, sib, z)
+        slab = slab_of(plane, by_y)
+        arrive(slab)
+        if step in (0, 3):
+            send(slab, by_x, z, part=1)
+        send(slab, sib, z)
+        for block in (b, by_x, by_y):
+            arrive(slab_of(plane, other_core(block)))
+            correlate(step, block)
+        if step < 3:
+            turn(step + 1)
+        if step == 0:
+            corner(0)
+        elif step == 2:
+            corner(1)
+    corner(2)
+    corner(3)
+
+    for copy in copies:
+        copy.wait()
+    for copy, when in sends:
+        if when is None:
+            copy.wait_send()
+        else:
+            pl.when(when)(copy.wait_send)
+
+
+def kernel_body(records, glitch_mask, fir_taps):
+    blocks, planes = lax.axis_size("blk"), lax.axis_size("tm")
+    tm_index = lax.axis_index("tm")
+    chans, segs, seglen = records.shape
+    seg_total = glitch_mask.shape[1]
+    lags_dev = LAGS // planes
+    depth = segs * 2 * BINS
+    usable = lax.dynamic_slice_in_dim(glitch_mask, tm_index * segs, segs, 1).astype(jnp.float32)
+    middle = (fir_taps.shape[0] - 1) // 2
+    back = fir_taps[::-1].astype(jnp.float32)
+    line = jnp.concatenate(
+        [back[middle:], jnp.zeros((2 * seglen - 2 * middle - 1,), jnp.float32), back[:middle]]
+    )[None, :]
+    bf16 = jnp.bfloat16
+    return pl.pallas_call(
+        kernel,
+        out_shape=jax.ShapeDtypeStruct((lags_dev, chans, chans * blocks), bf16),
+        in_specs=[pl.BlockSpec(memory_space=pltpu.VMEM)] * 5,
+        out_specs=pl.BlockSpec(memory_space=pl.ANY),
+        scratch_shapes=[
+            pltpu.VMEM((blocks * planes, chans, depth), bf16),
+            pltpu.VMEM((planes, lags_dev, chans, depth), bf16),
+            pltpu.VMEM((lags_dev, chans, chans * blocks), jnp.float32),
+            pltpu.VMEM((lags_dev, chans, chans * blocks), bf16),
+            pltpu.SemaphoreType.DMA((48,)),
+            pltpu.SemaphoreType.DMA((blocks * planes, 2)),
+            pltpu.SemaphoreType.DMA((4,)),
+        ],
+        compiler_params=pltpu.CompilerParams(
+            collective_id=0, has_side_effects=True, vmem_limit_bytes=58 * 1024 * 1024
+        ),
+        cost_estimate=pl.CostEstimate(
+            flops=2 * lags_dev * chans * chans * blocks * planes * depth,
+            bytes_accessed=2 * lags_dev * chans * chans * blocks,
+            transcendentals=0,
+        ),
+    )(
+        jnp.transpose(records, (1, 0, 2)),
+        usable,
+        line,
+        jnp.asarray(dft_thirds(seglen)),
+        jnp.asarray(lag_rows(seg_total, seglen)),
+    )
+
+
 def solution(mesh):
     placed = (P("blk", "tm", None), P("blk", None), P())
+    small = mesh.shape["blk"] == 8 and mesh.shape["tm"] == 4
     return jax.shard_map(
-        body, mesh=mesh, in_specs=placed, out_specs=P("tm", "blk", None), check_vma=False
-    )
+        kernel_body if small else gathered_body,
+        mesh=mesh,
+        in_specs=placed,
+        out_specs=P("tm", "blk", None),
+        check_vma=False,
+    )

time: 193 us -> 109 us (0.56)
  Pallas kernels: 0 us -> 98.8 us
  waiting for transfers between devices: 68 us -> 0 us
  other arithmetic: 41.5 us -> 1.34 us
  local copies, waits for them, and re-layouts: 40.2 us -> 8.16 us
  matrix products: 28.6 us -> 0 us
  between operations: 13.5 us -> 0.03 us
    pallas_call x0 -> x1, Pallas kernels: none -> 98.8 us  [kernel_body(): pl.pallas_call(kernel, out_shape=jax.ShapeDtypeStruct((lags_dev, chans, c...]
    all_gather x2 -> x0, waiting for transfers between devices: 67.9 us -> none  [the longest x1 48.6 us: body(): column = lax.all_gather(slab, 'tm', axis=1, tiled=True)]
    another operation x2 -> x0, other arithmetic: 39 us -> none  [the longest x1 20.3 us: body(): jnp.stack([cos_rows * real_part - sin_rows * imag_part, cos_rows * imag_p...]
    dot_general x3 -> x0, matrix products: 28.6 us -> none  [the longest x1 23.8 us: body(): jnp.einsum('lik,jk->lij', left, every, preferred_element_type=jnp.float32)]
    convert_element_type x6 -> x0, local copies, waits for them, and re-layouts: 24 us -> none  [the longest x1 14.5 us: body(): turned = jnp.stack([cos_rows * real_part - sin_rows * imag_part, cos_rows...]
    slice x1 -> x2, local copies, waits for them, and re-layouts: 10.3 us -> 0.08 us  [the longest x1 0.07 us: kernel_body(): back[middle:]]
    unnamed x2 -> x5, local copies, waits for them, and re-layouts: 0.52 us -> 7.31 us
    reshape x2 -> x0, local copies, waits for them, and re-layouts: 2.74 us -> none  [the longest x1 1.63 us: filter_matrix(): jnp.tile(line, seglen)[:seglen * (period - 1)].reshape(seglen, period - 1)]
  transfers between devices with their start and end apart: 2 -> 0, of which waited for: 2 -> 0; matrix products, arithmetic and copies ran while one was open for 37% -> 0% of each run, Pallas kernels for 0% -> 0%
where the time goes in v2:
time: 109 us; the launch traced here: 108 us
  Pallas kernels  98.8 us (91%)
  local copies, waits for them, and re-layouts  8.16 us (7%)
  other arithmetic  1.34 us (1%)
    pallas_call x1, Pallas kernels, kernel_body(): pl.pallas_call(kernel, out_shape=jax.ShapeDtypeStruct((lags_dev, chans, c...  98.8 us
    unnamed x5, local copies, waits for them, and re-layouts  7.31 us

profile of v2, /device:TPU:0, one launch (start us, length us, event | category | flops | bytes accessed | tf_op | source)
XLA Modules:
  0.0 108.3 jit_solution(694650997743927739)
XLA Ops:
  0.0 0.0 copy-start
  0.0 0.8 rev.3
  0.8 0.1 slice.6
  0.8 0.0 copy-done
  0.9 0.7 pad_maximum_fusion
  1.5 0.1 copy.8
  1.7 0.7 convert_element_type.6.use_ref
  2.3 2.4 %copy.10 = bf16[256,4,512]{2,0,1:T(8,128)(2,1)} copy(bf16[256,4,512]{2,1,0:T(4,128)(2,1)} %param.5) | data formatting | bytes 2097152 | tf_op args[0]
  4.7 98.8 %shard_map.55 = bf16[4,256,2048]{2,1,0:T(8,128)(2,1)} custom-call(bf16[4,256,512]{2,1,0:T(8,128)(2,1)} %bitcast.4, f32[256,4]{1,0:T(8,128)} %convert_element_type.6.use_ref, f32[1,1024]{1,0:T(1,128)} %bitcast.5, bf16[512,768]{1,0:T(8,128)(2,1)} %constant.16.clone.dft_ref, f32[2,16,128]{2,1,0:T(8,128)} %constant.17.clone.tab_ref), custom_call_target="tpu_custom_call" | custom-call | flops 17179869184 | bytes 4194304 | tf_op jit(solution)/shard_map/pallas_call | solution.py:324
  103.5 4.8 %copy.12 = bf16[4,256,2048]{2,1,0:T(8,128)(2,1)} copy(bf16[4,256,2048]{2,1,0:T(8,128)(2,1)} %shard_map.55) | data formatting | bytes 8388608
  (3 shorter events, 0.0 us)
Async XLA Ops:
  0.0 0.8 copy-start

commit v3 on v2

--- a/solution.py
+++ b/solution.py
@@ -12,6 +12,7 @@
 FIRST_BIN = 16
 SMOOTH = 64
 LAGS = 16
+GROUP = 4
 
 
 def dft_thirds(seglen):
@@ -147,7 +148,7 @@
     where = lax.broadcasted_iota(jnp.int32, (1, seglen), 1)
     counts = jnp.minimum(where, SMOOTH) + jnp.minimum(seglen - 1 - where, SMOOTH) + 1
     counts = counts.astype(jnp.float32)
-    for s in range(segs):
+    def whiten_segment(s):
         samples = x_ref[s]
         envelope = jnp.dot(jnp.abs(samples), band_ones, preferred_element_type=jnp.float32) / counts
         normal = (samples.astype(jnp.float32) / (envelope + 1e-06)).astype(jnp.bfloat16)
@@ -156,33 +157,34 @@
         scale = use_ref[:, s : s + 1] / jnp.sqrt(power + 1e-06)
         slabs[own, :, s * width : (s + 1) * width] = (spectra * scale).astype(jnp.bfloat16)
 
-    pl.semaphore_wait(barrier, 3 + has_up.astype(jnp.int32) + has_down.astype(jnp.int32))
-
-    sends = []
+    sends = {}
 
     def view(slab, part):
         if part is None:
             return slabs.at[slab], got.at[slab, 0]
+        if part >= 2:
+            columns = pl.ds((part - 2) * depth // 2, depth // 2)
+            return slabs.at[slab, :, columns], got.at[slab, 0]
         return slabs.at[slab, pl.ds(part * half, half)], got.at[slab, part]
 
-    def send(slab, block, plane, part=None, when=None):
+    def make(index, slab, block, plane, part):
         ref, sem = view(slab, part)
-        copy = pltpu.make_async_remote_copy(
-            src_ref=ref, dst_ref=ref, send_sem=sent.at[len(sends)], recv_sem=sem,
+        return pltpu.make_async_remote_copy(
+            src_ref=ref, dst_ref=ref, send_sem=sent.at[index], recv_sem=sem,
             device_id=(block, plane), device_id_type=MESH,
         )
-        sends.append((copy, when))
+
+    def send(name, slab, block, plane, part=None, when=None):
+        if name not in sends:
+            sends[name] = (len(sends), slab, block, plane, part, when)
+        go = make(*sends[name][:-1]).start
         if when is None:
-            copy.start()
+            go()
         else:
-            pl.when(when)(copy.start)
+            pl.when(when)(go)
 
     def arrive(slab, part=None):
-        ref, sem = view(slab, part)
-        pltpu.make_async_remote_copy(
-            src_ref=ref, dst_ref=ref, send_sem=sent.at[0], recv_sem=sem,
-            device_id=(sib, z), device_id_type=MESH,
-        ).wait_recv()
+        make(0, slab, sib, z, part).wait_recv()
 
     plane_at, onward, goes_on = [z], [None], [None]
     for step in range(1, 4):
@@ -220,20 +222,25 @@
         first_slab = slab_of(plane_at[step], pair * 2)
         columns = pl.ds(pl.multiple_of(pair * 2 * chans, 2 * chans), 2 * chans)
 
-        def one(lag, carry):
-            right = slabs[pl.ds(first_slab, 2)].reshape(2 * chans, depth)
+        right = slabs[pl.ds(first_slab, 2)].reshape(2 * chans, depth)
+
+        def one(at, carry):
+            some = pl.ds(at * GROUP, GROUP)
             term = lax.dot_general(
-                left[step, lag], right, (((1,), (1,)), ((), ())), preferred_element_type=jnp.float32
-            )
+                left[step, some].reshape(GROUP * chans, depth),
+                right,
+                (((1,), (1,)), ((), ())),
+                preferred_element_type=jnp.float32,
+            ).reshape(GROUP, chans, 2 * chans)
             if step == 0:
-                acc[lag, :, columns] = term
+                acc[some, :, columns] = term
             elif step < 3:
-                acc[lag, :, columns] += term
+                acc[some, :, columns] += term
             else:
-                done[lag, :, columns] = (acc[lag, :, columns] + term).astype(jnp.bfloat16)
+                done[some, :, columns] = (acc[some, :, columns] + term).astype(jnp.bfloat16)
             return carry
 
-        lax.fori_loop(0, lags, one, 0)
+        lax.fori_loop(0, lags // GROUP, one, 0)
         if step == 3:
             copy = pltpu.make_async_copy(
                 done.at[:, :, columns], out_ref.at[:, :, columns], outs.at[len(copies)]
@@ -244,67 +251,111 @@
     def other_core(block):
         return block + 1 - 2 * core
 
-    send(own, b, up, when=has_up)
-    send(own, b, down, when=has_down)
-    send(own, by_x, z)
-    send(own, by_y, z)
-    send(own, sib, z)
+    in_middle = jnp.logical_and(has_up, has_down)
+    at_end = jnp.logical_not(in_middle)
+    mine, xs, ys, corners = [
+        [slab_of(plane, block) for plane in plane_at] for block in (b, by_x, by_y, across)
+    ]
+    twins = {
+        key: [slab_of(plane, other_core(block)) for plane in plane_at]
+        for key, block in (("b", b), ("x", by_x), ("y", by_y), ("c", across))
+    }
+
+    def guarded(when, action):
+        if when is None:
+            action()
+        else:
+            pl.when(when)(action)
+
+    def along_z(step, when=None):
+        def action():
+            slab = mine[step]
+            arrive(slab)
+            send(("z", step), slab, b, onward[step], when=goes_on[step])
+            send(("x", step), slab, by_x, z)
+            send(("y", step), slab, by_y, z)
+            send(("s", step), slab, sib, z)
+
+        guarded(when, action)
+
+    def neighbours(step):
+        arrive(xs[step])
+        if step in (0, 3):
+            send(("xy", step), xs[step], by_y, z, part=0)
+        send(("xs", step), xs[step], sib, z)
+        arrive(ys[step])
+        if step in (0, 3):
+            send(("yx", step), ys[step], by_x, z, part=1)
+        send(("ys", step), ys[step], sib, z)
+
+    def corner(step, when=None):
+        def action():
+            slab = corners[step]
+            if step in (0, 3):
+                arrive(slab, 0)
+                arrive(slab, 1)
+            else:
+                arrive(slab)
+            if step == 0:
+                send(("cu",), slab, b, up, when=has_up)
+                send(("cd",), slab, b, down, when=has_down)
+            elif step == 1:
+                send(("cz",), slab, b, onward[1], when=goes_on[1])
+            send(("cs", step), slab, sib, z)
+
+        guarded(when, action)
+
+    def multiply(step, keys):
+        for key in keys:
+            arrive(twins[key][step])
+            correlate(step, {"b": b, "x": by_x, "y": by_y, "c": across}[key])
+
+    for part in range(2):
+        for segment in range(part * segs // 2, (part + 1) * segs // 2):
+            whiten_segment(segment)
+        if part == 0:
+            pl.semaphore_wait(barrier, 3 + has_up.astype(jnp.int32) + has_down.astype(jnp.int32))
+        early = 2 + part
+        send(("u", part), own, b, up, early, has_up)
+        send(("d", part), own, b, down, early, has_down)
+        send(("x", 0, part), own, by_x, z, early)
+        send(("y", 0, part), own, by_y, z, early)
+        send(("s", 0, part), own, sib, z, early)
     turn(0)
-
-    def corner(step):
-        slab = slab_of(plane_at[step], across)
-        if step in (0, 3):
-            arrive(slab, 0)
-            arrive(slab, 1)
-        else:
-            arrive(slab)
-        if step == 0:
-            send(slab, b, up, when=has_up)
-            send(slab, b, down, when=has_down)
-        elif step == 1:
-            send(slab, b, onward[1], when=goes_on[1])
-        send(slab, sib, z)
-        arrive(slab_of(plane_at[step], other_core(across)))
-        correlate(step, across)
-
-    for step in range(4):
-        plane = plane_at[step]
-        if step < 3:
-            slab = slab_of(plane_at[step + 1], b)
-            arrive(slab)
-            send(slab, b, onward[step + 1], when=goes_on[step + 1])
-            send(slab, by_x, z)
-            send(slab, by_y, z)
-            send(slab, sib, z)
-        slab = slab_of(plane, by_x)
-        arrive(slab)
-        if step in (0, 3):
-            send(slab, by_y, z, part=0)
-        send(slab, sib, z)
-        slab = slab_of(plane, by_y)
-        arrive(slab)
-        if step in (0, 3):
-            send(slab, by_x, z, part=1)
-        send(slab, sib, z)
-        for block in (b, by_x, by_y):
-            arrive(slab_of(plane, other_core(block)))
-            correlate(step, block)
-        if step < 3:
-            turn(step + 1)
-        if step == 0:
-            corner(0)
-        elif step == 2:
-            corner(1)
+    multiply(0, "b")
+    along_z(1)
+    along_z(2, in_middle)
+    neighbours(0)
+    turn(1)
+    multiply(0, "xy")
+    multiply(1, "b")
+    along_z(2, at_end)
+    along_z(3, in_middle)
+    corner(0)
+    turn(2)
+    multiply(0, "c")
+    neighbours(1)
+    along_z(3, at_end)
+    corner(1, in_middle)
+    multiply(1, "xy")
+    multiply(2, "b")
+    neighbours(2)
+    turn(3)
+    multiply(2, "xy")
+    multiply(3, "b")
+    corner(1, at_end)
+    multiply(1, "c")
+    neighbours(3)
+    multiply(3, "xy")
     corner(2)
+    multiply(2, "c")
     corner(3)
+    multiply(3, "c")
 
     for copy in copies:
         copy.wait()
-    for copy, when in sends:
-        if when is None:
-            copy.wait_send()
-        else:
-            pl.when(when)(copy.wait_send)
+    for index, slab, block, plane, part, when in sends.values():
+        guarded(when, make(index, slab, block, plane, part).wait_send)
 
 
 def kernel_body(records, glitch_mask, fir_taps):

time: 109 us -> 91.3 us (0.84)
  the two profiles are of different devices: /device:TPU:0 before, /device:TPU:17 now
where the time goes in v3:
time: 91.3 us; the launch traced here: 91 us
  Pallas kernels  81.5 us (89%)
  local copies, waits for them, and re-layouts  8.16 us (9%)
  other arithmetic  1.34 us (1%)
    pallas_call x1, Pallas kernels, kernel_body(): pl.pallas_call(kernel, out_shape=jax.ShapeDtypeStruct((lags_dev, chans, c...  81.5 us
    unnamed x5, local copies, waits for them, and re-layouts  7.31 us

profile of v3, /device:TPU:17, one launch (start us, length us, event | category | flops | bytes accessed | tf_op | source)
XLA Modules:
  0.0 91.0 jit_solution(6710090734335182600)
XLA Ops:
  0.0 0.0 copy-start
  0.0 0.8 rev.3
  0.8 0.1 slice.6
  0.8 0.0 copy-done
  0.9 0.7 pad_maximum_fusion
  1.5 0.1 copy.8
  1.7 0.7 convert_element_type.6.use_ref
  2.3 2.4 %copy.10 = bf16[256,4,512]{2,0,1:T(8,128)(2,1)} copy(bf16[256,4,512]{2,1,0:T(4,128)(2,1)} %param.5) | data formatting | bytes 2097152 | tf_op args[0]
  4.7 81.5 %shard_map.55 = bf16[4,256,2048]{2,1,0:T(8,128)(2,1)} custom-call(bf16[4,256,512]{2,1,0:T(8,128)(2,1)} %bitcast.4, f32[256,4]{1,0:T(8,128)} %convert_element_type.6.use_ref, f32[1,1024]{1,0:T(1,128)} %bitcast.5, bf16[512,768]{1,0:T(8,128)(2,1)} %constant.16.clone.dft_ref, f32[2,16,128]{2,1,0:T(8,128)} %constant.17.clone.tab_ref), custom_call_target="tpu_custom_call" | custom-call | flops 17179869184 | bytes 4194304 | tf_op jit(solution)/shard_map/pallas_call | solution.py:375
  86.3 4.8 %copy.12 = bf16[4,256,2048]{2,1,0:T(8,128)(2,1)} copy(bf16[4,256,2048]{2,1,0:T(8,128)(2,1)} %shard_map.55) | data formatting | bytes 8388608
  (3 shorter events, 0.0 us)
Async XLA Ops:
  0.0 0.8 copy-start
